TPU v7x, 256 devices: a whole 4x4x8 slice. The times are simulated.
256 devices in a mesh: grp: 8 (over x_hi, y), tile: 32 (over x_lo, z, core).
Axes of the slice: x: 4 (x_hi: 2, x_lo: 2; x = x_hi * 2 + x_lo), y: 4, z: 8, core: 2. Of those that a mesh axis runs over, the one named last changes fastest.
Arguments:
- center: int32 [8], replicated, may hold values from 0 to 7, each once
- pair_occ: int32 [16, 2], P('grp'), may hold values from 0 to 7
- slab_map: int32 [16], replicated, may hold values from 0 to 1791
- eps_occ: float32 [8], replicated, may hold values from -2 to -0.5
- eps_vir: float32 [1792], replicated, may hold values from 0.2 to 3
- vvvo: bfloat16 [8, 16, 1792, 1792], P('grp', None, 'tile'), may hold values from -0.0034179688 to 0.0034179688
- hole_amps: bfloat16 [8, 16, 1792, 200], P('grp', None, 'tile'), may hold values from -0.009765625 to 0.009765625
- pair_amps: bfloat16 [16, 1792, 1792], P('grp', 'tile'), may hold values from -6 to 6
- pair_ints: bfloat16 [16, 1792, 200], P('grp', 'tile'), may hold values from -6 to 6
Outputs:
- energy_rows: float32 [16, 1792], P(None, 'tile')
- energy_total: float32 [], replicated
Inputs may be any that keep to these rules, and one draw needn't show every extreme that they name: `center`: each of 0 to 7 appears once.
All inputs are finite; a program needn't handle non-finite values.
Results may differ from a plain program's by a relative error of at most 0.0003.
Values may be sent and summed in bfloat16 or wider, within the bound.
A program may use at most 128 MiB of HBM per device.

v0:
```python
import jax
import jax.numpy as jnp
from jax import lax
from jax.sharding import PartitionSpec as P


def from_root(value, axis, source):
    kept = jnp.where(lax.axis_index(axis) == source, value, 0).astype(value.dtype)
    return lax.psum(kept, axis)


def contract(left, right):
    return lax.dot_general(
        left, right, (((1,), (1,)), ((), ())), preferred_element_type=jnp.float32
    )


def select_value(table, position):
    return jnp.sum(jnp.where(jnp.arange(table.shape[0]) == position, table, 0.0))


def shards(center, pair_occ, slab_map, eps_occ, eps_vir, vvvo, hole_amps, pair_amps, pair_ints):
    occ_local = vvvo.shape[0]
    slab_rows = vvvo.shape[1]
    tile_cols = vvvo.shape[2]
    virt_all = eps_vir.shape[0]
    holes_all = hole_amps.shape[3]
    target = center[0]
    owner_group = target // occ_local
    local_row = target % occ_local
    integral_rows = lax.dynamic_index_in_dim(vvvo, local_row, 0, keepdims=False)
    hole_rows = lax.dynamic_index_in_dim(hole_amps, local_row, 0, keepdims=False)
    integral_rows, hole_rows = (
        from_root(integral_rows, "grp", owner_group),
        from_root(hole_rows, "grp", owner_group),
    )
    particle_mat = integral_rows.reshape(slab_rows * tile_cols, virt_all)
    hole_mat = hole_rows.reshape(slab_rows * tile_cols, holes_all)
    virt_index = jnp.arange(virt_all)
    slab_energy = jnp.sum(
        jnp.where(slab_map[:, None] == virt_index[None, :], eps_vir[None, :], 0.0), axis=1
    )
    tile_pos = lax.axis_index("tile")
    tile_energy = lax.dynamic_slice_in_dim(eps_vir, tile_pos * tile_cols, tile_cols)
    outer_denom = (-(slab_energy[:, None] + tile_energy[None, :])).reshape(-1)
    center_energy = select_value(eps_occ, target)
    occ_index = jnp.arange(eps_occ.shape[0])
    pair_energy = jnp.sum(
        jnp.where(pair_occ[:, :, None] == occ_index[None, None, :], eps_occ[None, None, :], 0.0),
        axis=2,
    )
    occ_sums = center_energy + pair_energy[:, 0] + pair_energy[:, 1]

    def contribute(energy_sum, amp_piece, int_piece, occ_total):
        triples = contract(particle_mat, amp_piece) - contract(hole_mat, int_piece)
        denominator = occ_total + outer_denom[:, None] - eps_vir[None, :]
        return energy_sum + jnp.sum(triples * triples / denominator, axis=1)

    running = jnp.zeros((slab_rows * tile_cols,), jnp.float32)
    for pair_slot in range(pair_amps.shape[0]):

        def add_pair(energy_sum, pieces, first_row, pair_slot=pair_slot):
            return contribute(energy_sum, pieces[0], pieces[1], occ_sums[pair_slot])

        running = add_pair(
            running,
            (
                lax.all_gather(pair_amps[pair_slot], "tile", axis=0, tiled=True),
                lax.all_gather(pair_ints[pair_slot], "tile", axis=0, tiled=True),
            ),
            jnp.int32(0),
        )
    energy_local = running.reshape(slab_rows, tile_cols)
    energy_rows = lax.psum(energy_local, "grp")
    energy_total = lax.psum(jnp.sum(energy_rows), "tile")
    return (energy_rows, energy_total)


def solution(mesh):
    in_specs = (
        P(),
        P("grp", None),
        P(),
        P(),
        P(),
        P("grp", None, "tile", None),
        P("grp", None, "tile", None),
        P("grp", "tile", None),
        P("grp", "tile", None),
    )
    out_specs = (P(None, "tile"), P())
    return jax.shard_map(shards, mesh=mesh, in_specs=in_specs, out_specs=out_specs, check_vma=False)
```

profile of v0, /device:TPU:1, one launch (start us, length us, event | category | flops | bytes accessed | tf_op | source)
XLA Modules:
  0.0 292.7 jit_solution(4487648483015689796)
XLA Ops:
  8.8 1.9 broadcast_select_fusion
  10.7 0.8 broadcast_select_fusion.1
  11.6 0.8 fusion.12
  12.5 0.5 all-gather.9.cloned.1.call-update
  13.1 0.6 fusion.11
  13.8 0.2 fusion.10
  13.9 0.7 slice_add_fusion
  14.6 0.5 fusion.14
  15.2 0.2 select_reduce_fusion
  15.4 1.4 fusion.8
  16.7 0.1 add.96
  16.8 0.1 add.99
  16.9 41.7 %all-gather.1 = bf16[1,1792,200]{2,1,0:T(8,128)(2,1)S(1)} all-gather(bf16[1,56,200]{2,1,0:T(8,128)(2,1)S(1)} %get-tuple-element.7), channel_id=3, replica_groups=mesh['grp'=8,'tile'=32] {'tile'}, dimensions={1}, use_global_device_ids=true | all-gather | bytes 739200 | tf_op jit(solution)/shard_map/all_gather | solution.py:69
  58.6 33.9 %all-gather.3 = bf16[1,1792,200]{2,1,0:T(8,128)(2,1)S(1)} all-gather(bf16[1,56,200]{2,1,0:T(8,128)(2,1)S(1)} %get-tuple-element.6), channel_id=5, replica_groups=mesh['grp'=8,'tile'=32] {'tile'}, dimensions={1}, use_global_device_ids=true | all-gather | bytes 739200 | tf_op jit(solution)/shard_map/all_gather | solution.py:69
  92.5 59.6 %all-reduce.3.cloned.1.call-done = (bf16[896,1792]{1,0:T(8,128)(2,1)}, bf16[896,200]{1,0:T(8,128)(2,1)}) async-done(((bf16[896,1792]{1,0:T(8,128)(2,1)}, bf16[896,200]{1,0:T(8,128)(2,1)}), (bf16[896,1792]{1,0:T(8,128)(2,1)}, bf16[896,200]{1,0:T(8,128)(2,1)})) %all-reduce.3.cloned.1.call-update) | async-done | bytes 3569680 | tf_op jit(solution)/shard_map/psum | solution.py:9
  152.0 10.0 %fusion.2 = f32[896,1792]{1,0:T(8,128)S(1)} fusion(bf16[896,1792]{1,0:T(8,128)(2,1)} %get-tuple-element.2, bf16[1,1792,1792]{2,1,0:T(8,128)(2,1)} %all-gather.7.cloned.1.call-done), kind=kOutput, calls=%fused_computation.2 | convolution fusion | flops 5754585088 | bytes 16056320 | tf_op jit(solution)/shard_map/dot_general | solution.py:13
  162.0 1.8 fusion.4
  163.8 33.1 %all-gather.9.cloned.1.call-done = bf16[1,1792,1792]{2,1,0:T(8,128)(2,1)} async-done(((bf16[1,56,1792]{2,1,0:T(8,128)(2,1)}), bf16[1,1792,1792]{2,1,0:T(8,128)(2,1)}) %all-gather.9.cloned.1.call-update) | async-done | bytes 6422544 | tf_op jit(solution)/shard_map/all_gather | solution.py:68
  197.0 9.8 %fusion = f32[896,1792]{1,0:T(8,128)S(1)} fusion(bf16[896,1792]{1,0:T(8,128)(2,1)} %get-tuple-element.2, bf16[1,1792,1792]{2,1,0:T(8,128)(2,1)} %all-gather.9.cloned.1.call-done), kind=kOutput, calls=%fused_computation | convolution fusion | flops 5754585088 | bytes 16056320 | tf_op jit(solution)/shard_map/dot_general | solution.py:13
  206.8 1.8 fusion.5
  208.6 0.1 add.101
  208.7 18.9 %psum.30 = f32[16,56]{1,0:T(8,128)S(1)} all-reduce(f32[16,56]{1,0:T(8,128)S(1)} %add.101), channel_id=1, replica_groups=mesh['grp'=8,'tile'=32] {'grp'}, use_global_device_ids=true, to_apply=%region_7.8 | all-reduce | flops 896 | bytes 7168 | tf_op jit(solution)/shard_map/psum | solution.py:74
  227.6 0.6 reduce_sum.59
  228.2 57.0 %psum.31 = f32[]{:T(128)} all-reduce(f32[]{:T(128)} %reduce_sum.59), channel_id=1, replica_groups=mesh['grp'=8,'tile'=32] {'tile'}, use_global_device_ids=true, to_apply=%region_9.10 | all-reduce | flops 1 | bytes 8 | tf_op jit(solution)/shard_map/psum | solution.py:75
  (29 shorter events, 0.3 us)
Async XLA Ops:
  8.0 5.1 %copy-start.9 = (s32[8]{0:T(128)S(1)}, s32[8]{0:T(128)}, u32[]{:S(2)}) copy-start(s32[8]{0:T(128)} %param.9) | copy-start | bytes 100
  8.0 2.7 copy-start
  8.0 3.6 %copy-start.1 = (bf16[2,56,1792]{2,1,0:T(8,128)(2,1)S(1)}, bf16[2,56,1792]{2,1,0:T(8,128)(2,1)}, u32[]{:S(2)}) copy-start(bf16[2,56,1792]{2,1,0:T(8,128)(2,1)} %param.16) | copy-start | bytes 1204228
  8.0 5.0 %copy-start.4 = (f32[1792]{0:T(1024)S(1)}, f32[1792]{0:T(1024)}, u32[]{:S(2)}) copy-start(f32[1792]{0:T(1024)} %param.13) | copy-start | bytes 21508
  8.0 5.1 %copy-start.6 = (f32[8]{0:T(128)S(1)}, f32[8]{0:T(128)}, u32[]{:S(2)}) copy-start(f32[8]{0:T(128)} %param.12) | copy-start | bytes 100
  8.0 5.7 %copy-start.5 = (s32[2,2]{1,0:T(2,128)S(1)}, s32[2,2]{1,0:T(2,128)}, u32[]{:S(2)}) copy-start(s32[2,2]{1,0:T(2,128)} %param.10) | copy-start | bytes 52
  8.1 7.1 %copy-start.7 = (s32[16]{0:T(128)S(1)}, s32[16]{0:T(128)}, u32[]{:S(2)}) copy-start(s32[16]{0:T(128)} %param.11) | copy-start | bytes 196
  8.1 8.8 %copy-start.2 = (bf16[2,56,200]{2,1,0:T(8,128)(2,1)S(1)}, bf16[2,56,200]{2,1,0:T(8,128)(2,1)}, u32[]{:S(2)}) copy-start(bf16[2,56,200]{2,1,0:T(8,128)(2,1)} %param.17) | copy-start | bytes 134404
  8.1 144.0 %all-reduce.3.cloned.1.call-start = ((), (), s32[]{:S(2)}) async-start(), calls=%async_computation.2 | async-start | bytes 7340032 | tf_op jit(solution)/shard_map/psum | solution.py:9
  11.6 140.5 %all-gather.7.cloned.1.call-start = ((), (), s32[]{:S(2)}) async-start(), calls=%async_computation | async-start | bytes 6623232 | tf_op jit(solution)/shard_map/all_gather | solution.py:68
  12.4 184.5 %all-gather.9.cloned.1.call-start = ((), (), s32[]{:S(2)}) async-start(), calls=%async_computation.1 | async-start | bytes 6623232 | tf_op jit(solution)/shard_map/all_gather | solution.py:68
  152.0 10.0 %copy-start.8 = (bf16[896,200]{1,0:T(8,128)(2,1)S(1)}, bf16[896,200]{1,0:T(8,128)(2,1)}, u32[]{:S(2)}) copy-start(bf16[896,200]{1,0:T(8,128)(2,1)} %get-tuple-element.3) | copy-start | bytes 1075204
  227.6 57.6 %copy-start.3 = (f32[16,56]{1,0:T(8,128)}, f32[16,56]{1,0:T(8,128)S(1)}, u32[]{:S(2)}) copy-start(f32[16,56]{1,0:T(8,128)S(1)} %psum.30) | copy-start | bytes 10756
Sparse Core Ops, SparseCore 0:
  11.7 140.2 all-reduce.2
Sparse Core Ops, SparseCore 1:
  13.9 103.0 all-gather.6
  118.7 78.2 all-gather.8
where the time goes:
time: 293 us
  blocking collectives  151 us (52%)
  waiting for transfers between devices  93.3 us (32%)
  matrix products  23.4 us (8%)
  between operations  16.4 us (6%)
  other arithmetic  6.39 us (2%)
    all_gather x2, blocking collectives, shards(): lax.all_gather(pair_ints[pair_slot], 'tile', axis=0, tiled=True)  75.5 us
    psum x1, waiting for transfers between devices, from_root(): return lax.psum(kept, axis)  59.6 us
    psum x1, blocking collectives, shards(): energy_total = lax.psum(jnp.sum(energy_rows), 'tile')  57 us
    all_gather x2, waiting for transfers between devices, shards(): lax.all_gather(pair_amps[pair_slot], 'tile', axis=0, tiled=True)  33.1 us
    dot_general x4, matrix products, contract(): lax.dot_general(left, right, (((1,), (1,)), ((), ())), preferred_element_...  23.4 us
    psum x1, blocking collectives, shards(): energy_rows = lax.psum(energy_local, 'grp')  18.9 us
  transfers between devices with their start and end apart: 3, of which 2 were waited for; matrix products, arithmetic and copies ran while one was open for 6% of the time, Pallas kernels for 0%

commit v1 on v0

v1 whole, which is shorter than its diff:
```python
import functools

import jax
import jax.numpy as jnp
from jax import lax
from jax.experimental import pallas as pl
from jax.experimental.pallas import tpu as pltpu
from jax.sharding import PartitionSpec as P

MESH = pl.DeviceIdType.MESH
DEPTH = 2048
CHUNK = 16
STEPS_ROWS = 14
MOVES = ((1, 0), (-1, 0), (0, 1), (0, -1))
PARENT = (
    (1, 2, 0, 3), (2, 0, 1, 3), (2, 0, 1, 3), (2, 0, 1, 3),
    (3, 1, 0, 2), (0, 1, 2, 3), (2, 1, 3, 0), (2, 1, 3, 0),
    (3, 1, 0, 2), (0, 1, 2, 3), (0, 3, 2, 1), (2, 3, 0, 1),
    (3, 1, 0, 2), (1, 2, 0, 3), (1, 2, 0, 3), (2, 3, 0, 1),
)


def tree_tables():
    def step(node, move, sign):
        return ((node // 4 + sign * move[0]) % 4) * 4 + (node % 4 + sign * move[1]) % 4

    depth = [[0] * 16 for _ in range(4)]
    child = [[0] * 4 for _ in range(4)]
    for tree in range(4):
        for node in range(1, 16):
            entered = PARENT[node][tree]
            child[tree][entered] |= 1 << step(node, MOVES[entered], -1)
            at, hops = node, 0
            while at != 0:
                at, hops = step(at, MOVES[PARENT[at][tree]], -1), hops + 1
            depth[tree][node] = hops
    planes = [[sum(((depth[t][v] >> b) & 1) << v for v in range(16)) for b in range(3)] for t in range(4)]
    return planes, child, max(max(d) for d in depth)


DEPTH_BITS, CHILD_BITS, DEEPEST = tree_tables()
STEPS = STEPS_ROWS + DEEPEST
RING_STEPS = (2, 4, 6, 8, 10, 12, 14)
SLOT_READY = (1, 4, 4, 8, 8, 12, 12, 14)
UNITS_PER_STEP = 5


def unit_schedule():
    units = sorted((max(2 * i + 1 + DEEPEST, SLOT_READY[o]), i, o) for i in range(7) for o in range(8))
    starts, at = [], 0
    for step in range(STEPS):
        starts.append(at)
        taken = 0
        while at < len(units) and units[at][0] <= step and (taken < UNITS_PER_STEP or step == STEPS - 1):
            at, taken = at + 1, taken + 1
    starts.append(at)
    assert at == len(units)
    codes = [i * 8 + o for _, i, o in units]
    words = [sum(c << (6 * n) for n, c in enumerate(codes[w : w + 5])) for w in range(0, len(codes), 5)]
    return starts, words


STARTS, WORDS = unit_schedule()


def pick(values, index):
    result = jnp.int32(values[0])
    for at in range(1, len(values)):
        if values[at] != values[at - 1]:
            result = jnp.where(index >= at, jnp.int32(values[at]), result)
    return result


def bit(mask, index):
    return jnp.bitwise_and(lax.shift_right_logical(jnp.int32(mask), index), 1)


def device(x, y, z, core):
    return (lax.div(x, 2) * 4 + y, lax.rem(x, 2) * 16 + z * 2 + core)


def kernel(
    owner, amps, rows, outer, col, out,
    mbuf, nbuf, obuf, acc, part, got1, got2,
    m_recv, m_send, z_recv, z_send, c_recv, c_send, local_sem, r1_recv, r1_send, r2_recv, r2_send,
):
    grp, tile = lax.axis_index("grp"), lax.axis_index("tile")
    y, x = lax.rem(grp, 4), lax.div(grp, 4) * 2 + lax.div(tile, 16)
    x_lo, z, core = lax.div(tile, 16), lax.div(lax.rem(tile, 16), 2), lax.rem(tile, 2)
    plane_pos = x * 4 + y
    tile0 = tile
    is_owner = grp == owner

    barrier = pltpu.get_barrier_semaphore()

    def plane_peer(n):
        pos = lax.rem(plane_pos + n, 16)
        return pos, device(lax.div(pos, 4), lax.rem(pos, 4), z, core)

    def tile_peer(n):
        pos = lax.rem(tile0 + n, 32)
        return pos, (grp, pos)

    def greet(peer_of):
        def one(n, carry):
            pl.semaphore_signal(barrier, inc=1, device_id=peer_of(n)[1], device_id_type=MESH)
            return carry

        return one

    lax.fori_loop(1, 16, greet(plane_peer), 0)
    lax.fori_loop(1, 32, greet(tile_peer), 0)

    own_rows = pltpu.make_async_copy(rows, mbuf.at[:, x_lo], local_sem.at[0])
    own_amps = pltpu.make_async_copy(amps, nbuf.at[z, pl.ds(pl.multiple_of(core * 112, 16), 112)], local_sem.at[1])
    pl.when(is_owner)(own_rows.start)
    own_amps.start()

    for slot in range(8):
        nbuf[slot, 224:256, :] = jnp.zeros((32, DEPTH), jnp.bfloat16)
    acc[...] = jnp.zeros_like(acc)
    part[...] = jnp.zeros_like(part)
    for n in range(14):
        line = jnp.broadcast_to(outer[n : n + 1, :], (128, 128))
        obuf[n // 2, (n % 2) * 128 : (n % 2) * 128 + 128, :] = line.T

    pl.semaphore_wait(barrier, 15 + 31)

    ahead = (device(x, y, lax.rem(z + 1, 8), core), device(x, y, lax.rem(z + 7, 8), core))
    sibling = device(x, y, z, 1 - core)
    piece = ((0, 64), (64, 48))

    def slot_of(p, d):
        return lax.rem(z + (8 - d if p == 0 else d), 8)

    def slot_rows(slot, whose, c):
        first, size = (0, 112) if c is None else piece[c]
        return nbuf.at[slot, pl.ds(pl.multiple_of(whose * 112 + first, 16), size)]


    def ring_send(p, d, c):
        first, size = piece[c]
        here = slot_rows(slot_of(p, d - 1), core, c)
        source = amps.at[pl.ds(first, size)] if d == 1 else here
        return pltpu.make_async_remote_copy(
            source, here, z_send.at[p, d - 1, c], z_recv.at[p, d - 1, c], device_id=ahead[p], device_id_type=MESH
        )

    def ring_got(p, d, c):
        here = slot_rows(slot_of(p, d), core, c)
        return pltpu.make_async_remote_copy(
            here, here, z_send.at[p, d - 1, c], z_recv.at[p, d - 1, c], device_id=ahead[p], device_id_type=MESH
        )

    def order_of(p, d):
        return 7 if d == 4 else (0 if d == 0 else 2 * d - 1 + p)

    def share(p, d, c):
        order = order_of(p, d)
        here = slot_rows(slot_of(p, d), core, c)
        source = amps if d == 0 else here
        n = 0 if c is None else c
        return pltpu.make_async_remote_copy(
            source, here, c_send.at[order, n], c_recv.at[order, n], device_id=sibling, device_id_type=MESH
        )

    def shared(p, d, c):
        order = order_of(p, d)
        here = slot_rows(slot_of(p, d), 1 - core, c)
        n = 0 if c is None else c
        return pltpu.make_async_remote_copy(
            here, here, c_send.at[order, n], c_recv.at[order, n], device_id=sibling, device_id_type=MESH
        )

    def travels(p, d, c):
        return d <= 3 or (d == 4 and p == c)

    for c in range(2):
        for p in range(2):
            ring_send(p, 1, c).start()
    share(0, 0, None).start()

    next_to = (
        device(lax.rem(x + 1, 4), y, z, core),
        device(lax.rem(x + 3, 4), y, z, core),
        device(x, lax.rem(y + 1, 4), z, core),
        device(x, lax.rem(y + 3, 4), z, core),
    )
    root_y, root_x = owner % 4, (owner // 4) * 2
    place = [lax.rem(x + 4 - root_x - s, 4) * 4 + lax.rem(y + 4 - root_y, 4) for s in range(2)]
    depth = [
        [sum(bit(DEPTH_BITS[t][b], place[s]) * (1 << b) for b in range(3)) for t in range(4)] for s in range(2)
    ]
    child = [[[bit(CHILD_BITS[t][d], place[s]) == 1 for d in range(4)] for t in range(4)] for s in range(2)]

    pl.when(is_owner)(own_rows.wait)
    own_amps.wait()

    def row_events(step):
        for t in range(4):
            for s in range(2):
                k = step - depth[s][t]

                @pl.when((k >= 0) & (k < STEPS_ROWS))
                def _(s=s, t=t, k=k):
                    q = 4 * k + t
                    part_rows = pl.ds(pl.multiple_of(lax.rem(q, 8) * CHUNK, CHUNK), CHUNK)
                    here = mbuf.at[lax.div(q, 8), s, part_rows]

                    def copy(d):
                        return pltpu.make_async_remote_copy(
                            here, here, m_send.at[s, t, d], m_recv.at[s, t, k],
                            device_id=next_to[d], device_id_type=MESH,
                        )

                    pl.when(place[s] != 0)(copy(0).wait_recv)
                    for d in range(4):
                        pl.when(child[s][t][d])(copy(d).start)

    def ring_event(n):
        d, c = (n // 2 + 1, n % 2) if n < 6 else (4, None)
        for p in range(2):
            cc = p if c is None else c
            ring_got(p, d, cc).wait_recv()
            if d < 4 and travels(p, d + 1, cc):
                ring_send(p, d + 1, cc).start()
            share(p, d, cc).start()

    def slots_shared(d):
        if d == 0:
            shared(0, 0, None).wait_recv()
        else:
            for p in range(2):
                for c in range(2):
                    if travels(p, d, c):
                        shared(p, d, c).wait_recv()

    def unit(u, carry):
        word = pick(WORDS, lax.div(u, 5))
        code = jnp.bitwise_and(lax.shift_right_logical(word, 6 * lax.rem(u, 5)), 63)
        i, o = lax.div(code, 8), lax.rem(code, 8)
        hops = lax.div(o + 1, 2)
        slot = lax.rem(jnp.where(lax.rem(o, 2) == 1, z + 8 - hops, z + hops), 8)
        left = mbuf[i].reshape(256, DEPTH)
        w = lax.dot_general(left, nbuf[slot], (((1,), (1,)), ((), ())), preferred_element_type=jnp.float32)
        base = obuf[i]
        line = col[pl.ds(slot, 1), :]
        total = acc[i]
        for h in range(2):
            wh = w[:, 128 * h : 128 * h + 128]
            total = total + wh * wh / (base + line[:, 128 * h : 128 * h + 128])
        acc[i] = total
        return carry

    def one_step(step, carry):
        row_events(step)
        for n, when in enumerate(RING_STEPS):
            pl.when(step == when)(functools.partial(ring_event, n))
        for d in range(5):
            pl.when(step == SLOT_READY[order_of(0, d)])(functools.partial(slots_shared, d))
        lax.fori_loop(pick(STARTS, step), pick(STARTS, step + 1), unit, 0)
        return carry

    lax.fori_loop(0, STEPS, one_step, 0)

    for n in range(14):
        block = acc[n // 2, (n % 2) * 128 : (n % 2) * 128 + 128, :]
        part[n % 2, n // 2 : n // 2 + 1, :] = jnp.sum(block.T, axis=0, keepdims=True)

    def first_copy(n):
        pos, peer = plane_peer(n)
        return pltpu.make_async_remote_copy(
            part.at[lax.rem(lax.div(pos, 4), 2)], got1.at[plane_pos], r1_send.at[n], r1_recv.at[plane_pos],
            device_id=peer, device_id_type=MESH,
        )

    def first_got(n):
        pos, peer = plane_peer(n)
        return pltpu.make_async_remote_copy(
            part.at[0], got1.at[pos], r1_send.at[n], r1_recv.at[pos], device_id=peer, device_id_type=MESH
        )

    def second_copy(n):
        pos, peer = tile_peer(n)
        return pltpu.make_async_remote_copy(
            got2.at[tile0], got2.at[tile0], r2_send.at[n], r2_recv.at[tile0], device_id=peer, device_id_type=MESH
        )

    def second_got(n):
        pos, peer = tile_peer(n)
        return pltpu.make_async_remote_copy(
            got2.at[pos], got2.at[pos], r2_send.at[n], r2_recv.at[pos], device_id=peer, device_id_type=MESH
        )

    def each(count, act):
        def one(n, carry):
            act(n)
            return carry

        lax.fori_loop(1, count, one, 0)

    each(16, lambda n: first_copy(n).start())
    got1[plane_pos] = part[x_lo]
    each(16, lambda n: first_got(n).wait_recv())
    summed = got1[0]
    for n in range(1, 16):
        summed = summed + got1[n]
    got2[tile0] = summed
    out[0:8, :] = summed
    each(32, lambda n: second_copy(n).start())

    each(16, lambda n: first_copy(n).wait_send())
    for s in range(2):
        for t in range(4):
            for d in range(4):

                @pl.when(child[s][t][d])
                def _(s=s, t=t, d=d):
                    whole = nbuf.at[0, pl.ds(0, STEPS_ROWS * CHUNK)]
                    pltpu.make_async_copy(whole, whole, m_send.at[s, t, d]).wait()

    share(0, 0, None).wait_send()
    for d in range(1, 5):
        for p in range(2):
            for c in range(2):
                if travels(p, d, c):
                    ring_send(p, d, c).wait_send()
                    share(p, d, c).wait_send()

    each(32, lambda n: second_got(n).wait_recv())
    everything = got2[0]
    for n in range(1, 32):
        everything = everything + got2[n]
    across = jnp.sum(everything, axis=1, keepdims=True)
    out[8:16, :] = jnp.broadcast_to(jnp.sum(across, axis=0, keepdims=True), (8, 128))
    each(32, lambda n: second_copy(n).wait_send())


def triples(owner, amps, rows, outer, col):
    bf16, f32 = jnp.bfloat16, jnp.float32
    return pl.pallas_call(
        functools.partial(kernel, owner),
        out_shape=jax.ShapeDtypeStruct((16, 128), f32),
        in_specs=[
            pl.BlockSpec(memory_space=pl.ANY),
            pl.BlockSpec(memory_space=pl.ANY),
            pl.BlockSpec(memory_space=pltpu.VMEM),
            pl.BlockSpec(memory_space=pltpu.VMEM),
        ],
        out_specs=pl.BlockSpec(memory_space=pltpu.VMEM),
        scratch_shapes=[
            pltpu.VMEM((7, 2, 128, DEPTH), bf16),
            pltpu.VMEM((8, 256, DEPTH), bf16),
            pltpu.VMEM((7, 256, 128), f32),
            pltpu.VMEM((7, 256, 128), f32),
            pltpu.VMEM((2, 8, 128), f32),
            pltpu.VMEM((16, 8, 128), f32),
            pltpu.VMEM((32, 8, 128), f32),
            pltpu.SemaphoreType.DMA((2, 4, STEPS_ROWS)),
            pltpu.SemaphoreType.DMA((2, 4, 4)),
            pltpu.SemaphoreType.DMA((2, 4, 2)),
            pltpu.SemaphoreType.DMA((2, 4, 2)),
            pltpu.SemaphoreType.DMA((8, 2)),
            pltpu.SemaphoreType.DMA((8, 2)),
            pltpu.SemaphoreType.DMA((2,)),
            pltpu.SemaphoreType.DMA((16,)),
            pltpu.SemaphoreType.DMA((16,)),
            pltpu.SemaphoreType.DMA((32,)),
            pltpu.SemaphoreType.DMA((32,)),
        ],
        compiler_params=pltpu.CompilerParams(
            collective_id=owner, has_side_effects=True, vmem_limit_bytes=48 << 20
        ),
        name="triples",
    )(amps, rows, outer, col)


def shards(center, pair_occ, slab_map, eps_occ, eps_vir, vvvo, hole_amps, pair_amps, pair_ints):
    virt_all = eps_vir.shape[0]
    tile = lax.axis_index("tile")
    x_lo, zc = tile // 16, tile % 16

    fill = DEPTH - 1792 - 200
    rows = jnp.concatenate(
        [vvvo[0].reshape(896, 1792), -hole_amps[0].reshape(896, 200), jnp.zeros((896, fill), jnp.bfloat16)], axis=1
    ).reshape(7, 128, DEPTH)
    amps = jnp.concatenate(
        [pair_amps.reshape(112, 1792), pair_ints.reshape(112, 200), jnp.zeros((112, fill), jnp.bfloat16)], axis=1
    )

    slab_energy = jnp.sum(jnp.where(slab_map[:, None] == jnp.arange(virt_all)[None, :], eps_vir[None, :], 0.0), axis=1)
    tile_energy = lax.dynamic_index_in_dim(eps_vir.reshape(2, 16, 56), zc, 1, keepdims=False)
    outer = -(slab_energy[None, :, None] + tile_energy[:, None, :])
    outer = outer.reshape(2, 7, 128).transpose(1, 0, 2).reshape(14, 128)
    outer = jnp.pad(outer, ((0, 2), (0, 0)))

    occ_index = jnp.arange(eps_occ.shape[0])
    center_energy = jnp.sum(jnp.where(occ_index == center[0], eps_occ, 0.0))
    pair_energy = jnp.sum(jnp.where(pair_occ[:, :, None] == occ_index, eps_occ, 0.0), axis=2)
    occ_sums = center_energy + pair_energy[:, 0] + pair_energy[:, 1]
    mine = lax.dynamic_index_in_dim(eps_vir.reshape(2, 8, 2, 1, 56), x_lo, 0, keepdims=False)
    col = (occ_sums[None, None, :, None] - mine).reshape(8, 224)
    col = jnp.pad(col, ((0, 0), (0, 32)), constant_values=-1.0)

    out = lax.switch(center[0], [functools.partial(triples, n) for n in range(8)], amps, rows, outer, col)
    return out[0:7].reshape(16, 56), out[8, 0]


def solution(mesh):
    in_specs = (
        P(),
        P("grp", None),
        P(),
        P(),
        P(),
        P("grp", None, "tile", None),
        P("grp", None, "tile", None),
        P("grp", "tile", None),
        P("grp", "tile", None),
    )
    out_specs = (P(None, "tile"), P())
    return jax.shard_map(shards, mesh=mesh, in_specs=in_specs, out_specs=out_specs, check_vma=False)
```

time: 293 us -> 123 us (0.42)
  blocking collectives: 151 us -> 0 us
  Pallas kernels: 0 us -> 108 us
  waiting for transfers between devices: 93.3 us -> 0 us
  matrix products: 23.4 us -> 0 us
  between operations: 16.4 us -> 0.87 us
  local copies, waits for them, and re-layouts: 1.67 us -> 9.5 us
    pallas_call x0 -> x1, Pallas kernels: none -> 108 us  [triples(): pl.pallas_call(functools.partial(kernel, owner), out_shape=jax.ShapeDtype...]
    psum x2 -> x0, blocking collectives: 75.9 us -> none  [the longest x1 57 us: shards(): energy_total = lax.psum(jnp.sum(energy_rows), 'tile')]
    all_gather x2 -> x0, blocking collectives: 75.5 us -> none  [shards(): lax.all_gather(pair_ints[pair_slot], 'tile', axis=0, tiled=True)]
    psum x1 -> x0, waiting for transfers between devices: 59.6 us -> none  [from_root(): return lax.psum(kept, axis)]
    all_gather x2 -> x0, waiting for transfers between devices: 33.1 us -> none  [shards(): lax.all_gather(pair_amps[pair_slot], 'tile', axis=0, tiled=True)]
    dot_general x4 -> x0, matrix products: 23.4 us -> none  [contract(): lax.dot_general(left, right, (((1,), (1,)), ((), ())), preferred_element_...]
    concatenate x0 -> x2, local copies, waits for them, and re-layouts: none -> 6.55 us  [the longest x1 6.45 us: shards(): jnp.concatenate([vvvo[0].reshape(896, 1792), -hole_amps[0].reshape(896, 2...]
  transfers between devices with their start and end apart: 3 -> 0, of which waited for: 2 -> 0; matrix products, arithmetic and copies ran while one was open for 6% -> 0% of each run, Pallas kernels for 0% -> 0%
where the time goes in v1:
time: 123 us; the launch traced here: 122 us
  Pallas kernels  108 us (88%)
  local copies, waits for them, and re-layouts  9.5 us (8%)
  other arithmetic  3.51 us (3%)
    pallas_call x1, Pallas kernels, triples(): pl.pallas_call(functools.partial(kernel, owner), out_shape=jax.ShapeDtype...  108 us
    concatenate x1, local copies, waits for them, and re-layouts, shards(): jnp.concatenate([vvvo[0].reshape(896, 1792), -hole_amps[0].reshape(896, 2...  6.45 us

profile of v1, /device:TPU:1, one launch (start us, length us, event | category | flops | bytes accessed | tf_op | source)
XLA Modules:
  0.0 122.4 jit_solution(4966198575327626346)
XLA Ops:
  0.6 0.8 reshape.55
  1.5 0.1 add.67
  1.5 0.9 select_reduce_fusion
  2.4 0.1 add.60
  2.5 0.1 add.61
  2.6 1.1 neg.11
  3.8 0.0 copy-start.1
  3.8 0.0 copy-start.2
  3.8 6.5 %concatenate.11 = bf16[7,128,2048]{2,1,0:T(8,128)(2,1)} concatenate(bf16[7,128,1792]{2,1,0:T(8,128)(2,1)} %bitcast.58, bf16[7,128,200]{2,1,0:T(8,128)(2,1)S(1)} %bitcast.59, bf16[7,128,56]{2,1,0:T(8,128)(2,1)S(1)} %broadcast_in_dim.39), dimensions={2} | concatenate | bytes 7340032 | tf_op jit(solution)/shard_map/concatenate | solution.py:384
  10.3 0.1 concatenate.9
  10.5 110.7 %conditional.1 = (f32[16,128]{1,0:T(8,128)S(1)}) conditional(s32[]{:T(128)} %clamp.3, (bf16[112,2048]{1,0:T(8,128)(2,1)S(1)}, bf16[7,128,2048]{2,1,0:T(8,128)(2,1)}, f32[7,2,128]{2,0,1:T(8,128)S(1)}, s32[8]{0:T(128)S(1)}, f32[]{:T(128)}, /*index=5*/f32[1792]{0:T(1024)S(1)}, s32[]{:T(128)}, s32[]{:T(128)}, ...), branch_computations={%region_3.4_spmd.clone.clone, %region_4.5_spmd.clone.clone, %regio... | conditional | flops 1919 | bytes 124383 | solution.py:405
  10.8 0.1 reshape.102
  10.9 0.1 sub.191
  11.0 0.2 fusion.15
  11.2 0.1 fusion.29
  11.2 0.1 copy.77
  11.3 0.1 copy.78
  11.4 0.7 fusion.16
  12.1 0.6 fusion.17
  12.8 0.1 sub.194
  12.8 0.1 sub.192
  13.0 108.2 %triples.13 = f32[16,128]{1,0:T(8,128)S(1)} custom-call(bf16[112,2048]{1,0:T(8,128)(2,1)S(1)} %get-tuple-element.1281.amps, bf16[7,128,2048]{2,1,0:T(8,128)(2,1)} %get-tuple-element.1282.rows, f32[16,128]{1,0:T(8,128)S(1)} %pad.52.outer, f32[8,256]{1,0:T(8,128)S(1)} %pad.53.col), custom_call_target="tpu_custom_call" | custom-call | tf_op jit(solution)/shard_map/cond/branch_5_fun/triples/pallas_call | solution.py:341
  121.2 0.7 reshape.58
  121.9 0.5 slice.20
  (25 shorter events, 0.2 us)
Async XLA Ops:
  3.8 6.5 %copy-start.1 = (bf16[2,56,1792]{2,1,0:T(8,128)(2,1)S(1)}, bf16[2,56,1792]{2,1,0:T(8,128)(2,1)}, u32[]{:S(2)}) copy-start(bf16[2,56,1792]{2,1,0:T(8,128)(2,1)} %param.24) | copy-start | bytes 1204228
  3.8 6.5 %copy-start.4 = (bf16[2,56,200]{2,1,0:T(8,128)(2,1)S(1)}, bf16[2,56,200]{2,1,0:T(8,128)(2,1)}, u32[]{:S(2)}) copy-start(bf16[2,56,200]{2,1,0:T(8,128)(2,1)} %param.25) | copy-start | bytes 134404
  3.8 6.6 %copy-start = (f32[1792]{0:T(1024)S(1)}, f32[1792]{0:T(1024)}, u32[]{:S(2)}) copy-start(f32[1792]{0:T(1024)} %param.21) | copy-start | bytes 21508
  3.8 6.6 %copy-start.2 = (f32[8]{0:T(128)S(1)}, f32[8]{0:T(128)}, u32[]{:S(2)}) copy-start(f32[8]{0:T(128)} %param.20) | copy-start | bytes 100
  3.8 6.6 %copy-start.3 = (s32[2,2]{1,0:T(2,128)S(1)}, s32[2,2]{1,0:T(2,128)}, u32[]{:S(2)}) copy-start(s32[2,2]{1,0:T(2,128)} %param.18) | copy-start | bytes 52
  3.8 6.6 %copy-start.5 = (s32[8]{0:T(128)S(1)}, s32[8]{0:T(128)}, u32[]{:S(2)}) copy-start(s32[8]{0:T(128)} %param.17) | copy-start | bytes 100

commit v2 on v0

v2 whole, which is shorter than its diff:
```python
import functools

import jax
import jax.numpy as jnp
from jax import lax
from jax.experimental import pallas as pl
from jax.experimental.pallas import tpu as pltpu
from jax.sharding import PartitionSpec as P

MESH = pl.DeviceIdType.MESH
DEPTH = 2048
CHUNK = 32
STEPS_ROWS = 14
MOVES = ((1, 0), (-1, 0), (0, 1), (0, -1))
PARENT = (
    (1, 2, 0, 3), (2, 0, 1, 3), (2, 0, 1, 3), (2, 0, 1, 3),
    (3, 1, 0, 2), (0, 1, 2, 3), (2, 1, 3, 0), (2, 1, 3, 0),
    (3, 1, 0, 2), (0, 1, 2, 3), (0, 3, 2, 1), (2, 3, 0, 1),
    (3, 1, 0, 2), (1, 2, 0, 3), (1, 2, 0, 3), (2, 3, 0, 1),
)


def tree_tables():
    def step(node, move, sign):
        return ((node // 4 + sign * move[0]) % 4) * 4 + (node % 4 + sign * move[1]) % 4

    depth = [[0] * 16 for _ in range(4)]
    child = [[0] * 4 for _ in range(4)]
    for tree in range(4):
        for node in range(1, 16):
            entered = PARENT[node][tree]
            child[tree][entered] |= 1 << step(node, MOVES[entered], -1)
            at, hops = node, 0
            while at != 0:
                at, hops = step(at, MOVES[PARENT[at][tree]], -1), hops + 1
            depth[tree][node] = hops
    planes = [[sum(((depth[t][v] >> b) & 1) << v for v in range(16)) for b in range(3)] for t in range(4)]
    return planes, child, max(max(d) for d in depth)


DEPTH_BITS, CHILD_BITS, DEEPEST = tree_tables()
LAG = 4
BLOCK_CHUNKS = 128 // CHUNK
FIRST_BLOCK = BLOCK_CHUNKS - 1 + LAG * DEEPEST
HALF_STEPS = FIRST_BLOCK + 6 * BLOCK_CHUNKS + 1
RING_STEPS = (7, 11, 16, 20, 25, 29, 33)
PAIR_READY = (12, 21, 30, 35)
UNITS_A_STEP = 1


def unit_schedule():
    units = sorted((max(FIRST_BLOCK + BLOCK_CHUNKS * i, PAIR_READY[o]), i, o) for i in range(7) for o in range(4))
    counts, at = [], 0
    for step in range(HALF_STEPS - 1):
        ready = sum(when <= step for when, _, _ in units)
        counts.append(min(ready - at, UNITS_A_STEP))
        at += counts[-1]
    counts.append(len(units) - at)
    assert max(counts) < 16
    runs = [sum(c << (4 * n) for n, c in enumerate(counts[w : w + 7])) for w in range(0, HALF_STEPS, 7)]
    codes = [i * 4 + o for _, i, o in units]
    words = [sum(c << (5 * n) for n, c in enumerate(codes[w : w + 6])) for w in range(0, len(codes), 6)]
    return runs, words


RUNS, WORDS = unit_schedule()


def pick(values, index):
    result = jnp.int32(values[0])
    for at in range(1, len(values)):
        if values[at] != values[at - 1]:
            result = jnp.where(index >= at, jnp.int32(values[at]), result)
    return result


def bit(mask, index):
    return jnp.bitwise_and(lax.shift_right_logical(jnp.int32(mask), index), 1)


def device(x, y, z, core):
    return (lax.div(x, 2) * 4 + y, lax.rem(x, 2) * 16 + z * 2 + core)


def kernel(
    owner, center, pair_occ, slab_map, eps_occ, eps_vir, eps_tiles, vvvo, hole, amps, ints, out,
    mbuf, nbuf, obuf, acc, colabs, col, part, got1, got2,
    m_recv, m_send, z_recv, z_send, c_recv, c_send, local_sem, f_recv, f_send,
):
    grp, tile = lax.axis_index("grp"), lax.axis_index("tile")
    x_lo, z, core = lax.div(tile, 16), lax.div(lax.rem(tile, 16), 2), lax.rem(tile, 2)
    y, x = lax.rem(grp, 4), lax.div(grp, 4) * 2 + x_lo
    plane_pos, line_pos = x * 4 + y, z * 2 + core
    is_owner = grp == owner

    def plane_peer(n):
        pos = lax.rem(plane_pos + n, 16)
        return pos, device(lax.div(pos, 4), lax.rem(pos, 4), z, core)

    def line_peer(n):
        pos = lax.rem(line_pos + n, 16)
        return pos, device(x, y, lax.div(pos, 2), lax.rem(pos, 2))

    own_rows = pltpu.make_async_copy(vvvo, mbuf.at[:, x_lo, :, pl.ds(0, 1792)], local_sem.at[0])
    own_amps = pltpu.make_async_copy(
        amps, nbuf.at[0, pl.ds(pl.multiple_of(core * 112, 16), 112), pl.ds(0, 1792)], local_sem.at[1]
    )
    pl.when(is_owner)(own_rows.start)
    own_amps.start()

    barrier = pltpu.get_barrier_semaphore()
    for peer_of in (plane_peer, line_peer):
        for n in range(1, 16):
            pl.semaphore_signal(barrier, inc=1, device_id=peer_of(n)[1], device_id_type=MESH)

    zeros = jnp.zeros((112, 56), jnp.bfloat16)
    own_half = pl.ds(pl.multiple_of(core * 112, 16), 112)
    nbuf[0, own_half, 1792:2048] = jnp.concatenate([-ints[...], zeros], axis=1)

    @pl.when(is_owner)
    def _():
        for i in range(7):
            filled = jnp.concatenate([hole[i], jnp.zeros((128, 56), jnp.bfloat16)], axis=1)
            mbuf[i, x_lo, :, 1792:2048] = filled

    lane = lax.broadcasted_iota(jnp.int32, (8, 128), 1)
    flat = lax.broadcasted_iota(jnp.int32, (8, 128), 0) * 128 + lane
    slab = lax.shift_right_logical(flat * 1171, 16)
    within = flat - slab * 56
    slab_part = jnp.zeros((8, 128), jnp.float32)
    for a in range(16):
        slab_part = jnp.where(slab == a, eps_vir[slab_map[a]], slab_part)
    for s in range(2):
        tile_part = jnp.zeros((8, 128), jnp.float32)
        for r in range(56):
            tile_part = jnp.where(within == r, eps_vir[(s * 16 + z * 2 + core) * 56 + r], tile_part)
        outer = -(slab_part + tile_part)
        for i in range(7):
            line = jnp.broadcast_to(outer[i : i + 1, :], (128, 128))
            obuf[i, s * 128 : s * 128 + 128, :] = line.T
    occ = [eps_occ[center[0]] + eps_occ[pair_occ[p, 0]] + eps_occ[pair_occ[p, 1]] for p in range(2)]
    even = eps_tiles[pl.ds(x_lo * 16, 8, stride=2), :]
    odd = eps_tiles[pl.ds(x_lo * 16 + 1, 8, stride=2), :]
    colabs[:, 0:128] = jnp.where(
        lane < 56,
        occ[0] - even,
        jnp.where(lane < 112, occ[1] - pltpu.roll(even, 56, 1), occ[0] - pltpu.roll(odd, 112, 1)),
    )
    colabs[:, 128:256] = jnp.where(
        lane < 40,
        occ[0] - pltpu.roll(odd, 112, 1),
        jnp.where(lane < 96, occ[1] - pltpu.roll(odd, 40, 1), -1.0),
    )
    for o in range(8):
        hops = (o + 1) // 2
        at = lax.rem(z + (8 - hops if o % 2 == 1 else hops), 8)
        col[o : o + 1, :] = colabs[pl.ds(at, 1), :]

    for slot in range(8):
        nbuf[slot, 224:256, :] = jnp.zeros((32, DEPTH), jnp.bfloat16)
    acc[...] = jnp.zeros_like(acc)
    part[...] = jnp.zeros_like(part)

    ahead = (device(x, y, lax.rem(z + 1, 8), core), device(x, y, lax.rem(z + 7, 8), core))
    sibling = device(x, y, z, 1 - core)
    piece = ((0, 64), (64, 48))

    def order_of(p, d):
        return 7 if d == 4 else (0 if d == 0 else 2 * d - 1 + p)

    def slot_rows(p, d, whose, c):
        first, size = (0, 112) if c is None else piece[c]
        return nbuf.at[order_of(p, d), pl.ds(pl.multiple_of(whose * 112 + first, 16), size)]

    def ring(p, d, c):
        return pltpu.make_async_remote_copy(
            slot_rows(p, d - 1, core, c), slot_rows(p, d, core, c), z_send.at[p, d - 1, c], z_recv.at[p, d - 1, c],
            device_id=ahead[p], device_id_type=MESH,
        )

    def share(p, d, c):
        here = slot_rows(p, d, core, c)
        sems = order_of(p, d), 0 if c is None else c
        return pltpu.make_async_remote_copy(
            here, here, c_send.at[sems], c_recv.at[sems], device_id=sibling, device_id_type=MESH
        )

    def shared(p, d, c):
        here = slot_rows(p, d, 1 - core, c)
        sems = order_of(p, d), 0 if c is None else c
        return pltpu.make_async_remote_copy(
            here, here, c_send.at[sems], c_recv.at[sems], device_id=sibling, device_id_type=MESH
        )

    def travels(p, d, c):
        return d <= 3 or (d == 4 and p == c)

    next_to = (
        device(lax.rem(x + 1, 4), y, z, core),
        device(lax.rem(x + 3, 4), y, z, core),
        device(x, lax.rem(y + 1, 4), z, core),
        device(x, lax.rem(y + 3, 4), z, core),
    )
    root_y, root_x = owner % 4, (owner // 4) * 2
    place = [lax.rem(x + 4 - root_x - s, 4) * 4 + lax.rem(y + 4 - root_y, 4) for s in range(2)]

    def of_core(table, j):
        return jnp.where(core == 0, jnp.int32(table[j]), jnp.int32(table[j + 2]))

    first_half = [
        [
            s + LAG * sum(bit(of_core([DEPTH_BITS[t][b] for t in range(4)], j), place[s]) * (1 << b) for b in range(3))
            for j in range(2)
        ]
        for s in range(2)
    ]
    child = [
        [[bit(of_core([CHILD_BITS[t][d] for t in range(4)], j), place[s]) == 1 for d in range(4)] for j in range(2)]
        for s in range(2)
    ]

    passes = [[child[s][j][0] | child[s][j][1] | child[s][j][2] | child[s][j][3] for j in range(2)] for s in range(2)]

    own_amps.wait()
    pl.semaphore_wait(barrier, 15 + 15)
    for c in range(2):
        for p in range(2):
            ring(p, 1, c).start()
    share(0, 0, None).start()
    pl.when(is_owner)(own_rows.wait)

    def row_events(half):
        for s in range(2):
            for j in range(2):
                since = half - first_half[s][j]

                @pl.when(passes[s][j] & (since >= 0) & (since < 2 * STEPS_ROWS) & (jnp.bitwise_and(since, 1) == 0))
                def _(s=s, j=j, since=since):
                    k = lax.shift_right_logical(since, 1)
                    q = since + j
                    part_rows = pl.ds(pl.multiple_of(lax.rem(q, BLOCK_CHUNKS) * CHUNK, CHUNK), CHUNK)
                    here = mbuf.at[lax.div(q, BLOCK_CHUNKS), s, part_rows]

                    def copy(d):
                        return pltpu.make_async_remote_copy(
                            here, here, m_send.at[s, j, d], m_recv.at[s, j, k],
                            device_id=next_to[d], device_id_type=MESH,
                        )

                    pl.when(place[s] != 0)(copy(0).wait_recv)
                    for d in range(4):
                        pl.when(child[s][j][d])(copy(d).start)

    def last_chunks(i):
        for s in range(2):
            for j in range(2):

                @pl.when(jnp.logical_not(passes[s][j]))
                def _(s=s, j=j):
                    for n in range(BLOCK_CHUNKS // 2):
                        here = mbuf.at[i, s, pl.ds((2 * n + j) * CHUNK, CHUNK)]
                        pltpu.make_async_remote_copy(
                            here, here, m_send.at[s, j, 0], m_recv.at[s, j, BLOCK_CHUNKS // 2 * i + n],
                            device_id=next_to[0], device_id_type=MESH,
                        ).wait_recv()

    def ring_event(n):
        d, c = (n // 2 + 1, n % 2) if n < 6 else (4, None)
        for p in range(2):
            cc = p if c is None else c
            ring(p, d, cc).wait_recv()
            if d < 4 and travels(p, d + 1, cc):
                ring(p, d + 1, cc).start()
            share(p, d, cc).start()

    def slots_shared(d):
        if d == 1:
            shared(0, 0, None).wait_recv()
        for p in range(2):
            for c in range(2):
                if travels(p, d, c):
                    shared(p, d, c).wait_recv()

    def unit(u, carry):
        word = pick(WORDS, lax.div(u, 6))
        code = jnp.bitwise_and(lax.shift_right_logical(word, 5 * lax.rem(u, 6)), 31)
        i, o = lax.div(code, 4), lax.rem(code, 4) * 2
        left = mbuf[i].reshape(256, DEPTH)
        right = nbuf[pl.ds(o, 2)].reshape(512, DEPTH)
        w = lax.dot_general(left, right, (((1,), (1,)), ((), ())), preferred_element_type=jnp.float32)
        base = obuf[i]
        total = acc[i]
        for n in range(2):
            line = col[pl.ds(o + n, 1), :]
            for h in range(2):
                wh = w[:, 256 * n + 128 * h : 256 * n + 128 * h + 128]
                total = total + wh * wh / (base + line[:, 128 * h : 128 * h + 128])
        acc[i] = total

        @pl.when(o == 6)
        def _():
            for s in range(2):
                across = jnp.sum(total[128 * s : 128 * s + 128, :].T, axis=0, keepdims=True)
                part[s, pl.ds(i, 1), :] = across

        return carry

    def one_half(half, done):
        row_events(half)
        for n, when in enumerate(RING_STEPS):
            pl.when(half == when)(functools.partial(ring_event, n))
        for d in range(1, 5):
            pl.when(half == PAIR_READY[d - 1])(functools.partial(slots_shared, d))
        block = half - FIRST_BLOCK

        @pl.when((block >= 0) & (lax.rem(block, BLOCK_CHUNKS) == 0))
        def _():
            last_chunks(lax.div(block, BLOCK_CHUNKS))

        word = lax.div(half, 7)
        runs = jnp.bitwise_and(lax.shift_right_logical(pick(RUNS, word), 4 * (half - 7 * word)), 15)
        lax.fori_loop(done, done + runs, unit, 0)
        return done + runs

    lax.fori_loop(0, HALF_STEPS, one_half, jnp.int32(0))

    local = jnp.sum(part[0] + part[1], axis=0, keepdims=True)
    part[0, 7:8, :] = local
    part[1, 7:8, :] = local

    def exchange(stage, got, own_pos, peer_of, source):
        for n in range(1, 16):
            pos, peer = peer_of(n)
            pltpu.make_async_remote_copy(
                source(pos), got.at[own_pos], f_send.at[stage], f_recv.at[stage], device_id=peer, device_id_type=MESH
            ).start()

    def settle(stage, got, sems):
        whole = got.at[pl.ds(0, 15)]
        pltpu.make_async_copy(whole, whole, sems.at[stage]).wait()

    exchange(0, got1, plane_pos, plane_peer, lambda pos: part.at[lax.rem(lax.div(pos, 4), 2)])
    got1[plane_pos] = part[x_lo]

    for s in range(2):
        for j in range(2):
            for d in range(4):

                @pl.when(child[s][j][d])
                def _(s=s, j=j, d=d):
                    whole = mbuf.at[:, 0, pl.ds(0, STEPS_ROWS * CHUNK // 7)]
                    pltpu.make_async_copy(whole, whole, m_send.at[s, j, d]).wait()

    share(0, 0, None).wait_send()
    for d in range(1, 5):
        for p in range(2):
            for c in range(2):
                if travels(p, d, c):
                    ring(p, d, c).wait_send()
                    share(p, d, c).wait_send()

    settle(0, got1, f_recv)
    rows = got1[0]
    for n in range(1, 16):
        rows = rows + got1[n]
    got2[line_pos] = rows
    exchange(1, got2, line_pos, line_peer, lambda pos: got2.at[line_pos])
    out[0:8, :] = rows
    settle(0, got1, f_send)
    settle(1, got2, f_recv)
    every = got2[0]
    for n in range(1, 16):
        every = every + got2[n]
    out[8:16, :] = jnp.broadcast_to(jnp.sum(every[7:8, :], axis=1, keepdims=True), (8, 128))
    settle(1, got2, f_send)


def triples(owner, *operands):
    bf16, f32 = jnp.bfloat16, jnp.float32
    smem, vmem = pl.BlockSpec(memory_space=pltpu.SMEM), pl.BlockSpec(memory_space=pltpu.VMEM)
    anywhere = pl.BlockSpec(memory_space=pl.ANY)
    return pl.pallas_call(
        functools.partial(kernel, owner),
        out_shape=jax.ShapeDtypeStruct((16, 128), f32),
        in_specs=[smem, smem, smem, smem, smem, vmem, anywhere, vmem, anywhere, vmem],
        out_specs=vmem,
        scratch_shapes=[
            pltpu.VMEM((7, 2, 128, DEPTH), bf16),
            pltpu.VMEM((8, 256, DEPTH), bf16),
            pltpu.VMEM((7, 256, 128), f32),
            pltpu.VMEM((7, 256, 128), f32),
            pltpu.VMEM((8, 256), f32),
            pltpu.VMEM((8, 256), f32),
            pltpu.VMEM((2, 8, 128), f32),
            pltpu.VMEM((16, 8, 128), f32),
            pltpu.VMEM((16, 8, 128), f32),
            pltpu.SemaphoreType.DMA((2, 2, STEPS_ROWS)),
            pltpu.SemaphoreType.DMA((2, 2, 4)),
            pltpu.SemaphoreType.DMA((2, 4, 2)),
            pltpu.SemaphoreType.DMA((2, 4, 2)),
            pltpu.SemaphoreType.DMA((8, 2)),
            pltpu.SemaphoreType.DMA((8, 2)),
            pltpu.SemaphoreType.DMA((2,)),
            pltpu.SemaphoreType.DMA((2,)),
            pltpu.SemaphoreType.DMA((2,)),
        ],
        compiler_params=pltpu.CompilerParams(
            collective_id=owner, has_side_effects=True, vmem_limit_bytes=48 << 20
        ),
        name="triples",
    )(*operands)


def shards(center, pair_occ, slab_map, eps_occ, eps_vir, vvvo, hole_amps, pair_amps, pair_ints):
    operands = (
        center,
        pair_occ,
        slab_map,
        eps_occ,
        eps_vir,
        jnp.pad(eps_vir.reshape(32, 56), ((0, 0), (0, 72))),
        vvvo.reshape(7, 128, 1792),
        hole_amps.reshape(7, 128, 200),
        pair_amps.reshape(112, 1792),
        pair_ints.reshape(112, 200),
    )
    out = lax.switch(center[0], [functools.partial(triples, n) for n in range(8)], *operands)
    return out[0:7].reshape(16, 56), out[8, 0]


def solution(mesh):
    in_specs = (
        P(),
        P("grp", None),
        P(),
        P(),
        P(),
        P("grp", None, "tile", None),
        P("grp", None, "tile", None),
        P("grp", "tile", None),
        P("grp", "tile", None),
    )
    out_specs = (P(None, "tile"), P())
    return jax.shard_map(shards, mesh=mesh, in_specs=in_specs, out_specs=out_specs, check_vma=False)
```

time: 293 us -> 91.6 us (0.31)
  blocking collectives: 151 us -> 0 us
  waiting for transfers between devices: 93.3 us -> 0 us
  Pallas kernels: 0 us -> 87.8 us
  matrix products: 23.4 us -> 0 us
  between operations: 16.4 us -> 1.29 us
  other arithmetic: 6.39 us -> 0 us
    pallas_call x0 -> x1, Pallas kernels: none -> 87.8 us  [triples(): pl.pallas_call(functools.partial(kernel, owner), out_shape=jax.ShapeDtype...]
    psum x2 -> x0, blocking collectives: 75.9 us -> none  [the longest x1 57 us: shards(): energy_total = lax.psum(jnp.sum(energy_rows), 'tile')]
    all_gather x2 -> x0, blocking collectives: 75.5 us -> none  [shards(): lax.all_gather(pair_ints[pair_slot], 'tile', axis=0, tiled=True)]
    psum x1 -> x0, waiting for transfers between devices: 59.6 us -> none  [from_root(): return lax.psum(kept, axis)]
    all_gather x2 -> x0, waiting for transfers between devices: 33.1 us -> none  [shards(): lax.all_gather(pair_amps[pair_slot], 'tile', axis=0, tiled=True)]
    dot_general x4 -> x0, matrix products: 23.4 us -> none  [contract(): lax.dot_general(left, right, (((1,), (1,)), ((), ())), preferred_element_...]
  transfers between devices with their start and end apart: 3 -> 0, of which waited for: 2 -> 0; matrix products, arithmetic and copies ran while one was open for 6% -> 0% of each run, Pallas kernels for 0% -> 0%
where the time goes in v2:
time: 91.6 us; the launch traced here: 91.4 us
  Pallas kernels  87.8 us (96%)
  local copies, waits for them, and re-layouts  1.98 us (2%)
  between operations  1.29 us (1%)
    pallas_call x1, Pallas kernels, triples(): pl.pallas_call(functools.partial(kernel, owner), out_shape=jax.ShapeDtype...  87.8 us

profile of v2, /device:TPU:1, one launch (start us, length us, event | category | flops | bytes accessed | tf_op | source)
XLA Modules:
  0.0 91.4 jit_solution(5860836127148447487)
XLA Ops:
  1.3 88.9 %conditional.1 = (f32[16,128]{1,0:T(8,128)S(1)}) conditional(s32[]{:T(128)} %bitcast, (s32[8]{0:T(128)}, s32[2,2]{1,0:T(2,128)}, s32[16]{0:T(128)}, f32[8]{0:T(128)}, f32[1792]{0:T(1024)}, /*index=5*/f32[1792]{0:T(1024)}, bf16[1,16,56,1792]{3,2,1,0:T(8,128)(2,1)}, bf16[1,16,56,200]{3,2,1,0:T(8,128)(2,1)}, ...), branch_computations={%region_0.1_spmd.clone, %region_1.2_spmd.clone, %region_2.3_spmd.c... | conditional | bytes 37900 | solution.py:427
  1.3 0.8 reshape.85
  2.1 87.8 %triples.10 = f32[16,128]{1,0:T(8,128)S(1)} custom-call(s32[8]{0:T(128)} %get-tuple-element.459.center, s32[2,2]{1,0:T(2,128)} %get-tuple-element.461.pair_occ, s32[16]{0:T(128)} %get-tuple-element.462.slab_map, f32[8]{0:T(128)} %get-tuple-element.463.eps_occ, f32[1792]{0:T(1024)} %get-tuple-element.464, f32[32,128]{1,0:T(8,128)S(1)} %pad.15.eps_tiles, ...), custom_call_target="tpu_custom_call" | custom-call | tf_op jit(solution)/shard_map/cond/branch_2_fun/triples/pallas_call | solution.py:382
  90.2 0.5 slice.11
  90.7 0.7 reshape.30
  (2 shorter events, 0.0 us)

commit v3 on v2

--- a/solution.py
+++ b/solution.py
@@ -43,13 +43,13 @@
 BLOCK_CHUNKS = 128 // CHUNK
 FIRST_BLOCK = BLOCK_CHUNKS - 1 + LAG * DEEPEST
 HALF_STEPS = FIRST_BLOCK + 6 * BLOCK_CHUNKS + 1
-RING_STEPS = (7, 11, 16, 20, 25, 29, 33)
-PAIR_READY = (12, 21, 30, 35)
-UNITS_A_STEP = 1
+RING_STEPS = (7, 11, 15, 19, 24, 28, 31)
+PAIR_READY = (12, 20, 29, 33)
+UNITS_A_STEP = 2
 
 
 def unit_schedule():
-    units = sorted((max(FIRST_BLOCK + BLOCK_CHUNKS * i, PAIR_READY[o]), i, o) for i in range(7) for o in range(4))
+    units = sorted((max(FIRST_BLOCK + BLOCK_CHUNKS * i, PAIR_READY[2 * o + 1]), i, o) for i in range(7) for o in range(2))
     counts, at = [], 0
     for step in range(HALF_STEPS - 1):
         ready = sum(when <= step for when, _, _ in units)
@@ -58,7 +58,7 @@
     counts.append(len(units) - at)
     assert max(counts) < 16
     runs = [sum(c << (4 * n) for n, c in enumerate(counts[w : w + 7])) for w in range(0, HALF_STEPS, 7)]
-    codes = [i * 4 + o for _, i, o in units]
+    codes = [i * 2 + o for _, i, o in units]
     words = [sum(c << (5 * n) for n, c in enumerate(codes[w : w + 6])) for w in range(0, len(codes), 6)]
     return runs, words
 
@@ -83,8 +83,8 @@
 
 
 def kernel(
-    owner, center, pair_occ, slab_map, eps_occ, eps_vir, eps_tiles, vvvo, hole, amps, ints, out,
-    mbuf, nbuf, obuf, acc, colabs, col, part, got1, got2,
+    owner, center, pair_occ, slab_map, eps_occ, eps_vir, eps_lines, vvvo, hole, amps, ints, out,
+    mbuf, nbuf, obuf, acc, tiles, colabs, col, part, got1, got2,
     m_recv, m_send, z_recv, z_send, c_recv, c_send, local_sem, f_recv, f_send,
 ):
     grp, tile = lax.axis_index("grp"), lax.axis_index("tile")
@@ -139,8 +139,16 @@
             line = jnp.broadcast_to(outer[i : i + 1, :], (128, 128))
             obuf[i, s * 128 : s * 128 + 128, :] = line.T
     occ = [eps_occ[center[0]] + eps_occ[pair_occ[p, 0]] + eps_occ[pair_occ[p, 1]] for p in range(2)]
-    even = eps_tiles[pl.ds(x_lo * 16, 8, stride=2), :]
-    odd = eps_tiles[pl.ds(x_lo * 16 + 1, 8, stride=2), :]
+    for n in range(16):
+        first = (x_lo * 16 + n) * 56
+        line, off = lax.div(first, 128), lax.rem(first, 128)
+        both = [
+            jnp.broadcast_to(eps_lines[pl.ds(lax.min(line + more, 13), 1), :], (8, 128)) for more in range(2)
+        ]
+        turned = [pltpu.roll(part_of, lax.rem(128 - off, 128), 1) for part_of in both]
+        here = jnp.where(lane + off < 128, turned[0], turned[1])
+        tiles[n % 2, n // 2 : n // 2 + 1, :] = here[0:1, :]
+    even, odd = tiles[0], tiles[1]
     colabs[:, 0:128] = jnp.where(
         lane < 56,
         occ[0] - even,
@@ -284,20 +292,20 @@
     def unit(u, carry):
         word = pick(WORDS, lax.div(u, 6))
         code = jnp.bitwise_and(lax.shift_right_logical(word, 5 * lax.rem(u, 6)), 31)
-        i, o = lax.div(code, 4), lax.rem(code, 4) * 2
+        i, o = lax.div(code, 2), lax.rem(code, 2) * 4
         left = mbuf[i].reshape(256, DEPTH)
-        right = nbuf[pl.ds(o, 2)].reshape(512, DEPTH)
+        right = nbuf[pl.ds(o, 4)].reshape(1024, DEPTH)
         w = lax.dot_general(left, right, (((1,), (1,)), ((), ())), preferred_element_type=jnp.float32)
         base = obuf[i]
         total = acc[i]
-        for n in range(2):
+        for n in range(4):
             line = col[pl.ds(o + n, 1), :]
             for h in range(2):
                 wh = w[:, 256 * n + 128 * h : 256 * n + 128 * h + 128]
                 total = total + wh * wh / (base + line[:, 128 * h : 128 * h + 128])
         acc[i] = total
 
-        @pl.when(o == 6)
+        @pl.when(o == 4)
         def _():
             for s in range(2):
                 across = jnp.sum(total[128 * s : 128 * s + 128, :].T, axis=0, keepdims=True)
@@ -389,6 +397,7 @@
             pltpu.VMEM((8, 256, DEPTH), bf16),
             pltpu.VMEM((7, 256, 128), f32),
             pltpu.VMEM((7, 256, 128), f32),
+            pltpu.VMEM((2, 8, 128), f32),
             pltpu.VMEM((8, 256), f32),
             pltpu.VMEM((8, 256), f32),
             pltpu.VMEM((2, 8, 128), f32),
@@ -418,7 +427,7 @@
         slab_map,
         eps_occ,
         eps_vir,
-        jnp.pad(eps_vir.reshape(32, 56), ((0, 0), (0, 72))),
+        eps_vir.reshape(14, 128),
         vvvo.reshape(7, 128, 1792),
         hole_amps.reshape(7, 128, 200),
         pair_amps.reshape(112, 1792),

time: 91.6 us -> 91.1 us (level)
  no operation moved by 1% of the time
where the time goes in v3:
time: 91.1 us; the launch traced here: 91 us
  Pallas kernels  87.9 us (96%)
  between operations  1.29 us (1%)
  local copies, waits for them, and re-layouts  1.2 us (1%)
    pallas_call x1, Pallas kernels, triples(): pl.pallas_call(functools.partial(kernel, owner), out_shape=jax.ShapeDtype...  87.9 us

profile of v3, /device:TPU:1, one launch (start us, length us, event | category | flops | bytes accessed | tf_op | source)
XLA Modules:
  0.0 91.0 jit_solution(13501024370944550820)
XLA Ops:
  1.3 88.5 %conditional.1 = (f32[16,128]{1,0:T(8,128)S(1)}) conditional(s32[]{:T(128)} %bitcast.40, (s32[8]{0:T(128)}, s32[2,2]{1,0:T(2,128)}, s32[16]{0:T(128)}, f32[8]{0:T(128)}, f32[1792]{0:T(1024)}, /*index=5*/f32[1792]{0:T(1024)}, bf16[1,16,56,1792]{3,2,1,0:T(8,128)(2,1)}, bf16[1,16,56,200]{3,2,1,0:T(8,128)(2,1)}, ...), branch_computations={%region_0.0_spmd, %region_1.0_spmd, %region_2.0_spmd, %region_3.0_... | conditional | bytes 8 | solution.py:436
  1.3 87.9 %triples.10 = f32[16,128]{1,0:T(8,128)S(1)} custom-call(s32[8]{0:T(128)} %get-tuple-element.189.center, s32[2,2]{1,0:T(2,128)} %get-tuple-element.317.pair_occ, s32[16]{0:T(128)} %get-tuple-element.325.slab_map, f32[8]{0:T(128)} %get-tuple-element.333.eps_occ, f32[1792]{0:T(1024)} %get-tuple-element.277, f32[14,128]{1,0:T(8,128)} %bitcast.77, ...), custom_call_target="tpu_custom_call" | custom-call | tf_op jit(solution)/shard_map/cond/branch_2_fun/triples/pallas_call | solution.py:390
  89.8 0.5 slice.11
  90.3 0.7 reshape.30
  (1 shorter events, 0.0 us)

commit v4 on v3

--- a/solution.py
+++ b/solution.py
@@ -43,9 +43,9 @@
 BLOCK_CHUNKS = 128 // CHUNK
 FIRST_BLOCK = BLOCK_CHUNKS - 1 + LAG * DEEPEST
 HALF_STEPS = FIRST_BLOCK + 6 * BLOCK_CHUNKS + 1
-RING_STEPS = (7, 11, 15, 19, 24, 28, 31)
-PAIR_READY = (12, 20, 29, 33)
-UNITS_A_STEP = 2
+RING_STEPS = (7, 10, 14, 17, 21, 25, 28)
+PAIR_READY = (12, 19, 27, 31)
+UNITS_A_STEP = 1
 
 
 def unit_schedule():

time: 91.1 us -> 90.2 us (level)
  no operation moved by 1% of the time
where the time goes in v4:
time: 90.2 us; the launch traced here: 90.1 us
  Pallas kernels  87.1 us (97%)
  between operations  1.29 us (1%)
  local copies, waits for them, and re-layouts  1.2 us (1%)
    pallas_call x1, Pallas kernels, triples(): pl.pallas_call(functools.partial(kernel, owner), out_shape=jax.ShapeDtype...  87.1 us

profile of v4, /device:TPU:1, one launch (start us, length us, event | category | flops | bytes accessed | tf_op | source)
XLA Modules:
  0.0 90.1 jit_solution(8362136946699713623)
XLA Ops:
  1.3 87.6 %conditional.1 = (f32[16,128]{1,0:T(8,128)S(1)}) conditional(s32[]{:T(128)} %bitcast.40, (s32[8]{0:T(128)}, s32[2,2]{1,0:T(2,128)}, s32[16]{0:T(128)}, f32[8]{0:T(128)}, f32[1792]{0:T(1024)}, /*index=5*/f32[1792]{0:T(1024)}, bf16[1,16,56,1792]{3,2,1,0:T(8,128)(2,1)}, bf16[1,16,56,200]{3,2,1,0:T(8,128)(2,1)}, ...), branch_computations={%region_0.0_spmd, %region_1.0_spmd, %region_2.0_spmd, %region_3.0_... | conditional | bytes 8 | solution.py:436
  1.3 87.1 %triples.9 = f32[16,128]{1,0:T(8,128)S(1)} custom-call(s32[8]{0:T(128)} %get-tuple-element.179.center, s32[2,2]{1,0:T(2,128)} %get-tuple-element.316.pair_occ, s32[16]{0:T(128)} %get-tuple-element.324.slab_map, f32[8]{0:T(128)} %get-tuple-element.332.eps_occ, f32[1792]{0:T(1024)} %get-tuple-element.276, f32[14,128]{1,0:T(8,128)} %bitcast.76, ...), custom_call_target="tpu_custom_call" | custom-call | tf_op jit(solution)/shard_map/cond/branch_1_fun/triples/pallas_call | solution.py:390
  88.9 0.5 slice.11
  89.4 0.7 reshape.30
  (1 shorter events, 0.0 us)
